TPU v7x, 256 devices: a whole 4x4x8 slice. The times are simulated.
256 devices in a mesh: dp: 8 (over y, core), tm: 32 (over z, x).
Axes of the slice: x: 4, y: 4, z: 8, core: 2. Of those that a mesh axis runs over, the one named last changes fastest.
Arguments:
- frames: bfloat16 [65536, 1536], P(('dp', 'tm')), may hold values from -28 to 28, as said below
- seg: int32 [8, 8192], P('dp'), may hold values from 0 to 3, never falling along the last dimension, each value on 1 to 4096 neighbouring positions
- look_back: int32 [8, 32], P('dp'), may hold values 0 or 1
- w_dw: float32 [5, 1536], replicated, may hold values from -2.5 to 2.5
- w_qkv: bfloat16 [1536, 4608], P(None, 'dp'), may hold values from -0.15625 to 0.15625
- w_o: bfloat16 [1536, 1536], replicated, may hold values from -1.5 to 1.5
- cotangent: bfloat16 [65536, 1536], P(('dp', 'tm')), may hold values from -1 to 1
Outputs:
- mixed: bfloat16 [65536, 1536], P(('dp', 'tm'))
- weight_grad: float32 [1536, 1536], P('tm', 'dp')
Inputs may be any that keep to these rules, and one draw needn't show every extreme that they name: Float features; a few short runs of frames may be several times larger than the rest. `seg`: recording numbers never fall along a replica's frames; each recording has 1 to 4096 frames, one exactly 4096.
All inputs are finite; a program needn't handle non-finite values. No bound on the sum of `look_back` on one device may be relied on, other than what follows from the above.
Results may differ from a plain program's by a relative error of at most 0.012.
The roundings to bfloat16 on the way count: a program that leaves them out, or rounds other values in their place, can miss the bound.
Values may be sent and summed in bfloat16 or wider, within the bound.
A program may use at most 128 MiB of HBM per device.

v0:
```python
import math
import jax
import jax.numpy as jnp
from jax import lax
from jax.sharding import PartitionSpec as P

KER = 5
STRETCH = 256


def extended(block, sides, width):
    for axis, dim in sides:
        count = lax.axis_size(axis)
        forward = [(i, i + 1) for i in range(count - 1)]
        backward = [(target, source) for source, target in forward]
        low = lax.ppermute(
            lax.slice_in_dim(block, block.shape[dim] - width, None, axis=dim), axis, forward
        )
        high = lax.ppermute(lax.slice_in_dim(block, 0, width, axis=dim), axis, backward)
        block = jnp.concatenate([low, block, high], axis=dim)
    return block


def swapped(block, axis, distance):
    count = lax.axis_size(axis)
    route = []
    for low in range(count):
        high = low | 1 << distance
        if high != low and high < count:
            route += [(low, high), (high, low)]
    return lax.ppermute(block, axis, route)


def stretch_attention(queries, keys, values, seg_row, look_row, stretch):
    frame_count, heads_here, head_dim = queries.shape
    value_dim = values.shape[2]
    blocks = frame_count // stretch
    query_blocks = queries.reshape(blocks, stretch, heads_here, head_dim)
    key_blocks = keys.reshape(blocks, stretch, heads_here, head_dim)
    value_blocks = values.reshape(blocks, stretch, heads_here, value_dim)
    key_pairs = jnp.concatenate(
        [jnp.concatenate([jnp.zeros_like(key_blocks[:1]), key_blocks[:-1]], 0), key_blocks], 1
    )
    value_pairs = jnp.concatenate(
        [jnp.concatenate([jnp.zeros_like(value_blocks[:1]), value_blocks[:-1]], 0), value_blocks], 1
    )
    seg_blocks = seg_row.reshape(blocks, stretch)
    seg_pairs = jnp.concatenate(
        [jnp.concatenate([jnp.full((1, stretch), -1, jnp.int32), seg_blocks[:-1]], 0), seg_blocks],
        1,
    )
    allow_prev = look_row == 1
    per_step = math.gcd(blocks, max(1, 512 // stretch))
    current = jnp.arange(2 * stretch) >= stretch
    scale = 1.0 / math.sqrt(head_dim)

    def block_step(block_index):
        start = block_index * per_step

        def pick_rows(array):
            return lax.dynamic_slice_in_dim(array, start, per_step, 0)

        scores = (
            jnp.einsum(
                "gqhd,gkhd->ghqk",
                pick_rows(query_blocks),
                pick_rows(key_pairs),
                preferred_element_type=jnp.float32,
            )
            * scale
        )
        same_rec = pick_rows(seg_pairs)[:, None, :] == pick_rows(seg_blocks)[:, :, None]
        allowed = same_rec & (current[None, None, :] | pick_rows(allow_prev)[:, None, None])
        scores = jnp.where(allowed[:, None], scores, -1e30)
        row_max = jnp.max(scores, axis=-1, keepdims=True)
        raw_weights = jnp.exp(scores - row_max)
        probs = (raw_weights / jnp.sum(raw_weights, axis=-1, keepdims=True)).astype(jnp.bfloat16)
        outputs = jnp.einsum(
            "ghqk,gkhv->gqhv", probs, pick_rows(value_pairs), preferred_element_type=jnp.float32
        )
        return outputs.astype(jnp.bfloat16).reshape(per_step * stretch, heads_here * value_dim)

    mixed = lax.map(block_step, jnp.arange(blocks // per_step, dtype=jnp.int32))
    return mixed.reshape(frame_count, heads_here * value_dim)


def local(frames, seg, look_back, w_dw, w_qkv, w_o, cotangent):
    rows = frames.shape[0]
    width = frames.shape[1]
    tm_count = lax.axis_size("tm")
    piece = width // tm_count
    half = KER // 2
    padded = extended(frames, (("tm", 0),), half)
    seg_row = seg[0]
    look_row = look_back[0]
    seg_padded = jnp.pad(seg_row, (half, half), constant_values=-1)
    local_seg = lax.dynamic_slice_in_dim(
        seg_padded, lax.axis_index("tm") * rows, rows + 2 * half, 0
    )
    own_seg = local_seg[half : half + rows]
    total = jnp.zeros((rows, width), jnp.float32)
    for offset in range(KER):
        same_rec = (local_seg[offset : offset + rows] == own_seg).astype(jnp.float32)
        total = (
            total
            + w_dw[offset] * padded[offset : offset + rows].astype(jnp.float32) * same_rec[:, None]
        )
    activ = jax.nn.silu(total).astype(jnp.bfloat16)
    qkv = jnp.dot(
        activ, lax.all_gather(w_qkv, "dp", axis=1, tiled=True), preferred_element_type=jnp.float32
    ).astype(jnp.bfloat16)
    arranged = qkv.reshape(rows, 3, tm_count, piece)
    arrived = lax.all_to_all(arranged, "tm", split_axis=2, concat_axis=0, tiled=True)
    frame_count = arrived.shape[0]
    lower = lax.axis_index("tm") % 2 == 0
    own_pair = arrived[:, 0:2, 0, :]
    other_pair = swapped(own_pair, "tm", 0)
    joined = jnp.where(
        lower,
        jnp.concatenate([own_pair, other_pair], -1),
        jnp.concatenate([other_pair, own_pair], -1),
    )
    queries = joined[:, 0][:, None, :]
    keys = joined[:, 1][:, None, :]
    values = arrived[:, 2, 0, :][:, None, :]
    attended = stretch_attention(queries, keys, values, seg_row, look_row, STRETCH)
    returned = lax.all_to_all(
        attended.reshape(frame_count, 1, piece), "tm", split_axis=0, concat_axis=1, tiled=True
    )
    attn = returned.reshape(rows, width)
    mixed = jnp.dot(attn, w_o, preferred_element_type=jnp.float32).astype(jnp.bfloat16)
    grad_term = lax.dot_general(
        attn, cotangent, (((0,), (0,)), ((), ())), preferred_element_type=jnp.float32
    )
    row_share = lax.psum_scatter(grad_term, "tm", scatter_dimension=0, tiled=True)
    weight_grad = lax.psum_scatter(row_share, "dp", scatter_dimension=1, tiled=True)
    return (mixed, weight_grad)


def solution(mesh):
    placed = (
        P(("dp", "tm"), None),
        P("dp", None),
        P("dp", None),
        P(),
        P(None, "dp"),
        P(),
        P(("dp", "tm"), None),
    )
    return jax.shard_map(
        local,
        mesh=mesh,
        in_specs=placed,
        out_specs=(P(("dp", "tm"), None), P("tm", "dp")),
        check_vma=False,
    )
```

profile of v0, /device:TPU:4, one launch (start us, length us, event | category | flops | bytes accessed | tf_op | source)
XLA Modules:
  0.0 700.8 jit_solution(11983358287464709644)
XLA Ops:
  8.4 2.4 collective-permute-start.1
  10.9 3.4 collective-permute-start
  14.6 2.0 collective-permute-done
  16.6 72.7 %all-gather.2.cloned.1.call-done = bf16[1536,4608]{0,1:T(8,128)(2,1)} async-done(((bf16[1536,576]{0,1:T(8,128)(2,1)}), bf16[1536,4608]{0,1:T(8,128)(2,1)}) %all-gather.2.cloned.1.call-update) | async-done | bytes 14155792 | tf_op jit(solution)/shard_map/all_gather | solution.py:110
  89.4 11.5 %convolution_convert_fusion.1 = bf16[256,4608]{1,0:T(8,128)(2,1)} fusion(bf16[1536,4608]{0,1:T(8,128)(2,1)} %all-gather.2.cloned.1.call-done, bf16[256,1536]{1,0:T(8,128)(2,1)S(1)} %copy-done.4, bf16[2,1536]{1,0:T(2,128)(2,1)S(1)} %collective-permute-done, bf16[258,1536]{1,0:T(8,128)(2,1)S(1)} %constant_dynamic-update-slice_fusion.1, ...), kind=kOutput, calls=%fused_computation.23 | convolution fusion | flops 3636461568 | bytes 18925568 | tf_op jit(solution)/shard_map/dot_general | solution.py:109
  100.8 2.8 copy.24
  103.8 66.5 %all_to_all.33 = bf16[256,3,32,48]{0,3,1,2:T(8,128)(2,1)S(1)} all-to-all(bf16[256,3,32,48]{0,3,1,2:T(8,128)(2,1)S(1)} %copy.25), channel_id=1, replica_groups=mesh['dp'=8,'tm'=32] {'tm'}, dimensions={2} | all-to-all | bytes 4718592 | tf_op jit(solution)/shard_map/all_to_all | solution.py:113
  170.6 1.3 slice_bitcast_fusion
  171.9 1.3 collective-permute-start.2
  177.0 1.6 fusion.13
  178.6 29.1 %collective-permute-done.2 = bf16[8192,2,48]{0,2,1:T(8,128)(2,1)} collective-permute-done((bf16[8192,2,48]{0,2,1:T(8,128)(2,1)}, bf16[8192,2,48]{0,2,1:T(8,128)(2,1)}, u32[]{:S(2)}, u32[]{:S(2)}) %collective-permute-start.2) | collective-permute-done | bytes 1572896 | tf_op jit(solution)/shard_map/ppermute | solution.py:31
  207.6 3.8 maximum_select_fusion
  211.7 1.3 slice.119
  213.0 1.6 copy.44
  214.6 3.6 slice.109
  218.2 1.6 copy.43
  220.6 2.9 fusion.11
  223.5 98.1 %while.11 = (s32[]{:T(128)}, bf16[16,512,48]{1,2,0:T(8,128)(2,1)S(1)}, s32[16]{0:T(128)S(1)}, bf16[32,512,1,48]{1,0,3,2:T(8,128)(2,1)}, s32[32,512]{1,0:T(8,128)...) while((s32[]{:T(128)}, ...), condition=%wide.region_3.4_spmd.clone, body=%wide.region_0.3_spmd.clone.sunk | while | flops 77621248 | bytes 3646681 | solution.py:83
  224.7 1.3 constant_dynamic-slice_fusion.12
  230.9 1.3 constant_dynamic-slice_fusion.12
  232.2 1.1 constant_dynamic-slice_fusion.13
  237.0 1.3 constant_dynamic-slice_fusion.12
  243.1 1.3 constant_dynamic-slice_fusion.12
  249.3 1.3 constant_dynamic-slice_fusion.12
  255.4 1.3 constant_dynamic-slice_fusion.12
  261.5 1.3 constant_dynamic-slice_fusion.12
  267.7 1.3 constant_dynamic-slice_fusion.12
  273.8 1.3 constant_dynamic-slice_fusion.12
  279.9 1.3 constant_dynamic-slice_fusion.12
  286.1 1.3 constant_dynamic-slice_fusion.12
  292.2 1.3 constant_dynamic-slice_fusion.12
  298.3 1.3 constant_dynamic-slice_fusion.12
  304.5 1.3 constant_dynamic-slice_fusion.12
  310.6 1.3 constant_dynamic-slice_fusion.12
  316.7 1.3 constant_dynamic-slice_fusion.12
  322.5 2.0 copy.34
  324.5 6.2 reshape.89
  331.2 45.2 %reduce.20 = bf16[8192,48]{1,0:T(8,128)(2,1)S(1)} reduce(bf16[8192,1,48]{2,1,0:T(2,128)(2,1)} %reshape.89, bf16[]{:T(256)} %broadcast.84), dimensions={1}, to_apply=%reshape.89.reduce_sub_computation | reduce | bytes 1572866 | tf_op jit(solution)/shard_map/reshape;reshape | solution.py:128
  376.4 4.2 reshape.107
  380.6 27.1 %all_to_all.34 = bf16[32,2,6144]{2,1,0:T(2,128)(2,1)S(1)} all-to-all(bf16[32,2,6144]{2,1,0:T(2,128)(2,1)} %reshape.107), channel_id=1, replica_groups=mesh['dp'=8,'tm'=32] {'tm'}, dimensions={0} | all-to-all | bytes 1572864 | tf_op jit(solution)/shard_map/all_to_all | solution.py:127
  407.7 7.9 %reshape.108 = bf16[8192,1,48]{2,1,0:T(2,128)(2,1)} reshape(bf16[32,2,6144]{2,1,0:T(2,128)(2,1)S(1)} %all_to_all.34) | data formatting | bytes 1572864
  415.5 8.1 %copy.32 = bf16[8192,1,48]{0,2,1:T(8,128)(2,1)S(1)} copy(bf16[8192,1,48]{2,1,0:T(2,128)(2,1)} %reshape.108) | data formatting | bytes 1572864 | tf_op jit(solution)/shard_map/all_to_all | solution.py:127
  424.3 5.0 fusion.34
  429.4 227.5 %reduce-scatter.5.cloned.1.call-done = f32[48,1536]{1,0:T(8,128)} async-done(((f32[1536,1536]{1,0:T(8,128)}), f32[48,1536]{1,0:T(8,128)}) %reduce-scatter.5.cloned.1.call-update) | async-done | bytes 294928 | tf_op jit(solution)/shard_map/reduce_scatter | solution.py:135
  656.9 2.1 copy.35
  659.1 4.6 convolution_convert_fusion.2
  663.7 29.0 %reduce-scatter.7.cloned.1.call-done = f32[192,48]{1,0:T(8,128)} async-done(((f32[1536,48]{1,0:T(8,128)}), f32[192,48]{1,0:T(8,128)}) %reduce-scatter.7.cloned.1.call-update) | async-done | bytes 36880
  692.7 1.6 copy.36
  (259 shorter events, 72.6 us)
Async XLA Ops:
  7.2 417.1 %copy-start = (bf16[256,1536]{1,0:T(8,128)(2,1)S(1)}, bf16[256,1536]{1,0:T(8,128)(2,1)}, u32[]{:S(2)}) copy-start(bf16[256,1536]{1,0:T(8,128)(2,1)} %param.15) | copy-start | bytes 2359300
  7.2 1.2 copy-start.4
  7.2 7.1 %copy-start.7 = (s32[1,8192]{1,0:T(1,128)S(1)}, s32[1,8192]{1,0:T(1,128)}, u32[]{:S(2)}) copy-start(s32[1,8192]{1,0:T(1,128)} %param.10) | copy-start | bytes 98308
  7.2 7.3 %copy-start.8 = (f32[5,1536]{1,0:T(8,128)S(1)}, f32[5,1536]{1,0:T(8,128)}, u32[]{:S(2)}) copy-start(f32[5,1536]{1,0:T(8,128)} %param.12) | copy-start | bytes 92164
  7.2 82.2 %all-gather.2.cloned.1.call-start = ((), (), s32[]{:S(2)}) async-start(), calls=%async_computation.4 | async-start | bytes 15925248 | tf_op jit(solution)/shard_map/all_gather | solution.py:110
  7.9 649.0 %reduce-scatter.5.cloned.1.call-start = ((), (), s32[]{:S(2)}) async-start(), calls=%async_computation.5 | async-start | bytes 9732096 | tf_op jit(solution)/shard_map/reduce_scatter | solution.py:135
  8.4 6.2 collective-permute-start.1
  10.9 5.8 collective-permute-start
  170.6 3.8 copy-start.9
  171.9 35.8 %collective-permute-start.2 = (bf16[8192,2,48]{0,2,1:T(8,128)(2,1)}, bf16[8192,2,48]{0,2,1:T(8,128)(2,1)}, u32[]{:S(2)}, u32[]{:S(2)}) collective-permute-start(bf16[8192,2,48]{0,2,1:T(8,128)(2,1)} %slice_bitcast_fusion), channel_id=1, source_target_pairs={{0,1},{1,0},{2,3},{3,2},{4,5},{5,4},{6,7},{7,6},{8,9},{9,8},{10,11... | collective-permute-start | bytes 4718600 | tf_op jit(solution)/shard_map/ppermute | solution.py:31
  175.4 1.1 copy-start.3
  218.2 1.6 copy-start.1
  218.2 2.4 copy-start.2
  220.6 2.9 copy-start.5
  321.6 0.9 copy-start.6
  429.3 263.3 %reduce-scatter.7.cloned.1.call-start = ((), (), s32[]{:S(2)}) async-start(), calls=%async_computation.6 | async-start | bytes 884736
Sparse Core Ops, SparseCore 0:
  9.9 79.4 all-gather.1
  429.5 227.4 reduce-scatter.4
  659.5 33.1 reduce-scatter.6
where the time goes:
time: 704 us; the launch traced here: 701 us
  waiting for transfers between devices  361 us (51%)
  local copies, waits for them, and re-layouts  121 us (17%)
  blocking collectives  93.6 us (13%)
  other arithmetic  55.5 us (8%)
  matrix products  36.9 us (5%)
  between operations  14 us (2%)
  loops' own time  11.7 us (2%)
  starting transfers between devices  7.23 us (1%)
    reduce_scatter x1, waiting for transfers between devices, local(): lax.psum_scatter(grad_term, 'tm', scatter_dimension=0, tiled=True)  228 us
    all_gather x1, waiting for transfers between devices, local(): lax.all_gather(w_qkv, 'dp', axis=1, tiled=True)  72.7 us
    all_to_all x1, blocking collectives, local(): lax.all_to_all(arranged, 'tm', split_axis=2, concat_axis=0, tiled=True)  66.5 us
    dynamic_slice x96, local copies, waits for them, and re-layouts, pick_rows(): return lax.dynamic_slice_in_dim(array, start, per_step, 0)  58.5 us
    another operation x1, other arithmetic, local(): attended.reshape(frame_count, 1, piece)  45.2 us
    unnamed x4, waiting for transfers between devices  29.7 us
    ppermute x1, waiting for transfers between devices, swapped(): return lax.ppermute(block, axis, route)  29.1 us
    all_to_all x1, blocking collectives, local(): lax.all_to_all(attended.reshape(frame_count, 1, piece), 'tm', split_axis=...  27.1 us
  transfers between devices with their start and end apart: 6, of which 5 were waited for; matrix products, arithmetic and copies ran while one was open for 1% of the time, Pallas kernels for 0%

commit v1 on v0

--- a/solution.py
+++ b/solution.py
@@ -110,7 +110,10 @@
         activ, lax.all_gather(w_qkv, "dp", axis=1, tiled=True), preferred_element_type=jnp.float32
     ).astype(jnp.bfloat16)
     arranged = qkv.reshape(rows, 3, tm_count, piece)
-    arrived = lax.all_to_all(arranged, "tm", split_axis=2, concat_axis=0, tiled=True)
+    arrived = jnp.concatenate(
+        lax.all_to_all(jnp.stack(jnp.split(arranged, lax.axis_size("tm"), axis=2)), "tm", 0, 0),
+        axis=0,
+    )
     frame_count = arrived.shape[0]
     lower = lax.axis_index("tm") % 2 == 0
     own_pair = arrived[:, 0:2, 0, :]

time: 704 us -> 704 us (level)
    unnamed x30 -> x59, local copies, waits for them, and re-layouts: 22.9 us -> 21.8 us
  transfers between devices with their start and end apart: 6 -> 6, of which waited for: 5 -> 5; matrix products, arithmetic and copies ran while one was open for 1% -> 2% of each run, Pallas kernels for 0% -> 0%
where the time goes in v1:
time: 704 us; the launch traced here: 701 us
  waiting for transfers between devices  360 us (51%)
  local copies, waits for them, and re-layouts  122 us (17%)
  blocking collectives  93.6 us (13%)
  other arithmetic  55.5 us (8%)
  matrix products  36.9 us (5%)
  between operations  14.3 us (2%)
  loops' own time  11.7 us (2%)
  starting transfers between devices  7.23 us (1%)
    reduce_scatter x1, waiting for transfers between devices, local(): lax.psum_scatter(grad_term, 'tm', scatter_dimension=0, tiled=True)  228 us
    all_gather x1, waiting for transfers between devices, local(): lax.all_gather(w_qkv, 'dp', axis=1, tiled=True)  72.4 us
    all_to_all x1, blocking collectives, local(): lax.all_to_all(jnp.stack(jnp.split(arranged, lax.axis_size('tm'), axis=2)...  66.5 us
    dynamic_slice x96, local copies, waits for them, and re-layouts, pick_rows(): return lax.dynamic_slice_in_dim(array, start, per_step, 0)  58.5 us
    another operation x1, other arithmetic, local(): attended.reshape(frame_count, 1, piece)  45.2 us
    unnamed x4, waiting for transfers between devices  29.7 us
    ppermute x1, waiting for transfers between devices, swapped(): return lax.ppermute(block, axis, route)  28.7 us
    all_to_all x1, blocking collectives, local(): lax.all_to_all(attended.reshape(frame_count, 1, piece), 'tm', split_axis=...  27.1 us
  transfers between devices with their start and end apart: 6, of which 5 were waited for; matrix products, arithmetic and copies ran while one was open for 2% of the time, Pallas kernels for 0%

profile of v1, /device:TPU:4, one launch (start us, length us, event | category | flops | bytes accessed | tf_op | source)
XLA Modules:
  0.0 701.1 jit_solution(7414366926172145263)
XLA Ops:
  8.8 2.4 collective-permute-start.1
  11.2 3.4 collective-permute-start
  15.7 1.3 collective-permute-done
  17.0 72.4 %all-gather.2.cloned.1.call-done = bf16[1536,4608]{0,1:T(8,128)(2,1)} async-done(((bf16[1536,576]{0,1:T(8,128)(2,1)}), bf16[1536,4608]{0,1:T(8,128)(2,1)}) %all-gather.2.cloned.1.call-update) | async-done | bytes 14155792 | tf_op jit(solution)/shard_map/all_gather | solution.py:110
  89.4 11.5 %convolution_convert_fusion.1 = bf16[256,4608]{1,0:T(8,128)(2,1)} fusion(bf16[1536,4608]{0,1:T(8,128)(2,1)} %all-gather.2.cloned.1.call-done, bf16[256,1536]{1,0:T(8,128)(2,1)S(1)} %copy-done.3, bf16[2,1536]{1,0:T(2,128)(2,1)S(1)} %collective-permute-done, bf16[258,1536]{1,0:T(8,128)(2,1)S(1)} %constant_dynamic-update-slice_fusion.1, ...), kind=kOutput, calls=%fused_computation.23 | convolution fusion | flops 3636461568 | bytes 18925568 | tf_op jit(solution)/shard_map/dot_general | solution.py:109
  100.8 2.8 copy.116
  104.2 66.5 %all_to_all.20 = bf16[32,256,3,1,48]{1,4,2,3,0:T(8,128)(2,1)S(1)} all-to-all(bf16[32,256,3,1,48]{1,4,2,3,0:T(8,128)(2,1)S(1)} %fusion.29), channel_id=1, replica_groups=mesh['dp'=8,'tm'=32] {'tm'}, dimensions={0} | all-to-all | bytes 4718592 | tf_op jit(solution)/shard_map/all_to_all | solution.py:114
  170.9 1.3 slice_bitcast_fusion
  172.2 1.3 collective-permute-start.2
  175.9 1.8 slice.102
  177.7 1.6 fusion.13
  179.3 28.7 %collective-permute-done.2 = bf16[8192,2,48]{0,2,1:T(8,128)(2,1)} collective-permute-done((bf16[8192,2,48]{0,2,1:T(8,128)(2,1)}, bf16[8192,2,48]{0,2,1:T(8,128)(2,1)}, u32[]{:S(2)}, u32[]{:S(2)}) %collective-permute-start.2) | collective-permute-done | bytes 1572896 | tf_op jit(solution)/shard_map/ppermute | solution.py:31
  208.0 3.8 maximum_select_fusion
  212.1 1.3 slice.119
  213.3 1.6 copy.196
  214.9 3.6 slice.109
  218.5 1.6 copy.195
  220.9 2.9 fusion.11
  223.8 98.1 %while.11 = (s32[]{:T(128)}, bf16[16,512,48]{1,2,0:T(8,128)(2,1)S(1)}, s32[16]{0:T(128)S(1)}, bf16[32,512,1,48]{1,0,3,2:T(8,128)(2,1)}, s32[32,512]{1,0:T(8,128)...) while((s32[]{:T(128)}, ...), condition=%wide.region_3.4_spmd.clone, body=%wide.region_0.3_spmd.clone.sunk | while | flops 77621248 | bytes 3646681 | solution.py:83
  225.1 1.3 constant_dynamic-slice_fusion.12
  231.2 1.3 constant_dynamic-slice_fusion.12
  237.3 1.3 constant_dynamic-slice_fusion.12
  243.5 1.3 constant_dynamic-slice_fusion.12
  249.6 1.3 constant_dynamic-slice_fusion.12
  255.7 1.3 constant_dynamic-slice_fusion.12
  261.9 1.3 constant_dynamic-slice_fusion.12
  268.0 1.3 constant_dynamic-slice_fusion.12
  274.1 1.3 constant_dynamic-slice_fusion.12
  280.3 1.3 constant_dynamic-slice_fusion.12
  286.4 1.3 constant_dynamic-slice_fusion.12
  292.5 1.3 constant_dynamic-slice_fusion.12
  298.7 1.3 constant_dynamic-slice_fusion.12
  304.8 1.3 constant_dynamic-slice_fusion.12
  310.9 1.3 constant_dynamic-slice_fusion.12
  317.1 1.3 constant_dynamic-slice_fusion.12
  322.8 2.0 copy.156
  324.8 6.2 reshape.93
  331.5 45.2 %reduce.20 = bf16[8192,48]{1,0:T(8,128)(2,1)S(1)} reduce(bf16[8192,1,48]{2,1,0:T(2,128)(2,1)} %reshape.93, bf16[]{:T(256)} %broadcast.84), dimensions={1}, to_apply=%reshape.93.reduce_sub_computation | reduce | bytes 1572866 | tf_op jit(solution)/shard_map/reshape;reshape | solution.py:131
  376.7 4.2 reshape.111
  380.9 27.1 %all_to_all.21 = bf16[32,2,6144]{2,1,0:T(2,128)(2,1)S(1)} all-to-all(bf16[32,2,6144]{2,1,0:T(2,128)(2,1)} %reshape.111), channel_id=1, replica_groups=mesh['dp'=8,'tm'=32] {'tm'}, dimensions={0} | all-to-all | bytes 1572864 | tf_op jit(solution)/shard_map/all_to_all | solution.py:130
  408.0 7.9 %reshape.112 = bf16[8192,1,48]{2,1,0:T(2,128)(2,1)} reshape(bf16[32,2,6144]{2,1,0:T(2,128)(2,1)S(1)} %all_to_all.21) | data formatting | bytes 1572864
  415.9 8.1 %copy.154 = bf16[8192,1,48]{0,2,1:T(8,128)(2,1)S(1)} copy(bf16[8192,1,48]{2,1,0:T(2,128)(2,1)} %reshape.112) | data formatting | bytes 1572864 | tf_op jit(solution)/shard_map/all_to_all | solution.py:130
  424.6 5.0 fusion.66
  429.7 227.5 %reduce-scatter.5.cloned.1.call-done = f32[48,1536]{1,0:T(8,128)} async-done(((f32[1536,1536]{1,0:T(8,128)}), f32[48,1536]{1,0:T(8,128)}) %reduce-scatter.5.cloned.1.call-update) | async-done | bytes 294928 | tf_op jit(solution)/shard_map/reduce_scatter | solution.py:138
  657.3 2.1 copy.157
  659.4 4.6 convolution_convert_fusion.2
  664.0 28.9 %reduce-scatter.7.cloned.1.call-done = f32[192,48]{1,0:T(8,128)} async-done(((f32[1536,48]{1,0:T(8,128)}), f32[192,48]{1,0:T(8,128)}) %reduce-scatter.7.cloned.1.call-update) | async-done | bytes 36880
  693.0 1.6 copy.158
  (288 shorter events, 73.5 us)
Async XLA Ops:
  7.2 417.5 %copy-start = (bf16[256,1536]{1,0:T(8,128)(2,1)S(1)}, bf16[256,1536]{1,0:T(8,128)(2,1)}, u32[]{:S(2)}) copy-start(bf16[256,1536]{1,0:T(8,128)(2,1)} %param.15) | copy-start | bytes 2359300
  7.2 8.3 %copy-start.3 = (bf16[256,1536]{1,0:T(8,128)(2,1)S(1)}, bf16[256,1536]{1,0:T(8,128)(2,1)}, u32[]{:S(2)}) copy-start(bf16[256,1536]{1,0:T(8,128)(2,1)} %param.9) | copy-start | bytes 2359300
  7.2 8.4 %copy-start.7 = (f32[5,1536]{1,0:T(8,128)S(1)}, f32[5,1536]{1,0:T(8,128)}, u32[]{:S(2)}) copy-start(f32[5,1536]{1,0:T(8,128)} %param.12) | copy-start | bytes 92164
  7.2 82.2 %all-gather.2.cloned.1.call-start = ((), (), s32[]{:S(2)}) async-start(), calls=%async_computation.4 | async-start | bytes 15925248 | tf_op jit(solution)/shard_map/all_gather | solution.py:110
  7.9 649.3 %reduce-scatter.5.cloned.1.call-start = ((), (), s32[]{:S(2)}) async-start(), calls=%async_computation.5 | async-start | bytes 9732096 | tf_op jit(solution)/shard_map/reduce_scatter | solution.py:138
  8.8 6.9 collective-permute-start.1
  11.2 5.8 collective-permute-start
  170.9 3.0 copy-start.6
  170.9 3.8 copy-start.8
  172.2 35.8 %collective-permute-start.2 = (bf16[8192,2,48]{0,2,1:T(8,128)(2,1)}, bf16[8192,2,48]{0,2,1:T(8,128)(2,1)}, u32[]{:S(2)}, u32[]{:S(2)}) collective-permute-start(bf16[8192,2,48]{0,2,1:T(8,128)(2,1)} %slice_bitcast_fusion), channel_id=1, source_target_pairs={{0,1},{1,0},{2,3},{3,2},{4,5},{5,4},{6,7},{7,6},{8,9},{9,8},{10,11... | collective-permute-start | bytes 4718600 | tf_op jit(solution)/shard_map/ppermute | solution.py:31
  218.5 1.6 copy-start.1
  218.5 2.4 copy-start.2
  220.9 2.9 copy-start.4
  321.9 0.9 copy-start.5
  429.7 263.3 %reduce-scatter.7.cloned.1.call-start = ((), (), s32[]{:S(2)}) async-start(), calls=%async_computation.6 | async-start | bytes 884736
Sparse Core Ops, SparseCore 0:
  9.9 79.4 all-gather.1
  429.8 227.4 reduce-scatter.4
  659.8 33.1 reduce-scatter.6
